TPU v7x, 256 devices: a whole 4x4x8 slice. The times are simulated.
256 devices in a mesh: dp: 16 (over x, z_lo), shard: 16 (over z_hi, y, core).
Axes of the slice: x: 4, y: 4, z: 8 (z_hi: 2, z_lo: 4; z = z_hi * 4 + z_lo), core: 2. Of those that a mesh axis runs over, the one named last changes fastest.
Arguments:
- patches: bfloat16 [32768, 3072], P(('dp', 'shard')), may hold values from -16.8 to 16.8
- query_cot: bfloat16 [32768, 4096], P('dp', 'shard'), may hold values from -5.1439285 to 5.1439285
- master: float32 [3072, 4096], P('dp', 'shard'), may hold values from -3 to 3
- moment: float32 [3072, 4096], P('dp', 'shard'), may hold values from -1.2 to 1.2
- second: float32 [3072, 4096], P('dp', 'shard'), may hold values from 0.25 to 4
Outputs:
- new_weight: bfloat16 [3072, 4096], P(None, 'shard')
- new_master: float32 [3072, 4096], P('dp', 'shard')
- new_moment: float32 [3072, 4096], P('dp', 'shard')
- new_second: float32 [3072, 4096], P('dp', 'shard')
All inputs are finite; a program needn't handle non-finite values.
Results may differ from a plain program's by a relative error of at most 0.007.
Values may be sent and summed in bfloat16 or wider, within the bound.
A program may use at most 192 MiB of HBM per device.

v0:
```python
import jax
import jax.numpy as jnp
from jax import lax
from jax.sharding import PartitionSpec as P

D = 3072
HEAD = 128
QW = 4096


MOMENT_FIX = 0.9999734386011124
SECOND_FIX = 0.994079470779666


def head_backward(query, cot_block):
    rows = query.shape[0]
    grouped = query.reshape(rows, -1, HEAD)
    centre = jnp.mean(grouped, axis=2, keepdims=True)
    spread = jnp.mean((grouped - centre) ** 2, axis=2, keepdims=True)
    rstd = 1.0 / jnp.sqrt(spread + 1e-06)
    normed = (grouped - centre) * rstd
    upper = cot_block.astype(jnp.float32).reshape(rows, -1, HEAD)
    inner = jnp.mean(upper * normed, axis=2, keepdims=True)
    dquery = rstd * (upper - jnp.mean(upper, axis=2, keepdims=True) - normed * inner)
    return dquery.reshape(rows, -1).astype(jnp.bfloat16)


def contract_rows(left, right):
    return lax.dot_general(
        left, right, (((0,), (0,)), ((), ())), preferred_element_type=jnp.float32
    )


def on_device(patches, query_cot, master, moment, second):
    weight0_part = master.astype(jnp.bfloat16)
    weight0 = lax.all_gather(weight0_part, "dp", axis=0, tiled=True)
    replica_rows = lax.all_gather(patches, "shard", axis=0, tiled=True)

    def local_grad(weight):
        query = jnp.dot(replica_rows, weight, preferred_element_type=jnp.float32)
        return contract_rows(replica_rows, head_backward(query, query_cot))

    grad1 = local_grad(weight0)
    target = jnp.sqrt(jnp.float32(D * QW))
    grad1_part = lax.psum_scatter(grad1, "dp", scatter_dimension=0, tiled=True)
    total = lax.psum(jnp.sum(grad1_part * grad1_part), ("dp", "shard"))
    scale = target / jnp.sqrt(total + 1e-12)
    tilted_part = (weight0_part.astype(jnp.float32) + scale * grad1_part).astype(jnp.bfloat16)
    weight1 = lax.all_gather(tilted_part, "dp", axis=0, tiled=True)
    grad2 = lax.psum_scatter(local_grad(weight1), "dp", scatter_dimension=0, tiled=True)
    new_moment = 0.9 * moment + 0.1 * grad2
    new_second = 0.95 * second + 0.05 * grad2 * grad2
    update = new_moment / MOMENT_FIX / (jnp.sqrt(new_second / SECOND_FIX) + 1e-08) + 0.1 * master
    new_master = master - 0.05 * update
    new_weight = lax.all_gather(new_master.astype(jnp.bfloat16), "dp", axis=0, tiled=True)
    return (new_weight, new_master, new_moment, new_second)


def solution(mesh):
    in_specs = (
        P(("dp", "shard"), None),
        P("dp", "shard"),
        P("dp", "shard"),
        P("dp", "shard"),
        P("dp", "shard"),
    )
    out_specs = (P(None, "shard"), P("dp", "shard"), P("dp", "shard"), P("dp", "shard"))
    return jax.shard_map(
        on_device, mesh=mesh, in_specs=in_specs, out_specs=out_specs, check_vma=False
    )
```

profile of v0, /device:TPU:8, one launch (start us, length us, event | category | flops | bytes accessed | tf_op | source)
XLA Modules:
  0.0 717.3 jit_solution(3328797051509988737)
XLA Ops:
  7.2 1.6 convert_element_type.22
  8.9 0.7 all-gather.5.cloned.1.call-update
  9.6 1.5 copy.29
  11.1 87.0 %all-gather.7.cloned.1.call-done = bf16[3072,256]{1,0:T(8,128)(2,1)} async-done(((bf16[192,256]{1,0:T(8,128)(2,1)}), bf16[3072,256]{1,0:T(8,128)(2,1)}) %all-gather.7.cloned.1.call-update) | async-done | bytes 1572880 | tf_op jit(solution)/shard_map/all_gather | solution.py:36
  98.1 141.5 %all-gather.5.cloned.1.call-done = bf16[2048,3072]{1,0:T(8,128)(2,1)} async-done(((bf16[128,3072]{1,0:T(8,128)(2,1)}), bf16[2048,3072]{1,0:T(8,128)(2,1)}) %all-gather.5.cloned.1.call-update) | async-done | bytes 12582928 | tf_op jit(solution)/shard_map/all_gather | solution.py:37
  239.6 6.9 bitcast_reduce_fusion.2
  246.8 0.5 bitcast_reduce_fusion.1
  247.3 0.5 fusion.2
  247.9 9.7 %convolution_bitcast_fusion.1 = f32[3072,256]{0,1:T(8,128)} fusion(bf16[2048,256]{0,1:T(8,128)(2,1)S(1)} %fusion.2, bf16[2048,3072]{1,0:T(8,128)(2,1)} %all-gather.5.cloned.1.call-done), kind=kOutput, calls=%fused_computation.1 | convolution fusion | flops 3221225472 | bytes 16777216 | tf_op jit(solution)/shard_map/dot_general | solution.py:29
  257.6 3.6 copy.34
  261.2 91.9 %reduce-scatter.7.cloned.1.call-done = f32[192,256]{1,0:T(8,128)} async-done(((f32[3072,256]{1,0:T(8,128)}), f32[192,256]{1,0:T(8,128)}) %reduce-scatter.7.cloned.1.call-update) | async-done | bytes 196624 | tf_op jit(solution)/shard_map/reduce_scatter | solution.py:45
  353.1 1.1 copy.35
  354.1 0.7 multiply_reduce_fusion.2
  354.8 73.7 %psum.7 = f32[]{:T(128)} all-reduce(f32[]{:T(128)} %multiply_reduce_fusion.2), channel_id=1, replica_groups=mesh['dp'=16,'shard'=16] {'dp','shard'}, use_global_device_ids=true, to_apply=%region_6.0 | all-reduce | flops 1 | bytes 8 | tf_op jit(solution)/shard_map/psum | solution.py:46
  429.2 1.6 add_convert_fusion
  431.0 81.1 %all-gather.9.cloned.1.call-done = bf16[3072,256]{1,0:T(8,128)(2,1)} async-done(((bf16[192,256]{1,0:T(8,128)(2,1)}), bf16[3072,256]{1,0:T(8,128)(2,1)}) %all-gather.9.cloned.1.call-update) | async-done | bytes 1572880 | tf_op jit(solution)/shard_map/all_gather | solution.py:49
  512.1 7.0 bitcast_reduce_fusion
  519.8 0.5 fusion.5
  520.3 6.4 convolution_bitcast_fusion
  526.7 2.4 copy.36
  529.2 95.2 %reduce-scatter.9.cloned.1.call-done = f32[192,256]{1,0:T(8,128)} async-done(((f32[3072,256]{1,0:T(8,128)}), f32[192,256]{1,0:T(8,128)}) %reduce-scatter.9.cloned.1.call-update) | async-done | bytes 196624 | tf_op jit(solution)/shard_map/reduce_scatter | solution.py:50
  624.4 1.9 fusion.9
  626.2 81.6 %all-gather.11.cloned.1.call-done = bf16[3072,256]{1,0:T(8,128)(2,1)} async-done(((bf16[192,256]{1,0:T(8,128)(2,1)}), bf16[3072,256]{1,0:T(8,128)(2,1)}) %all-gather.11.cloned.1.call-update) | async-done | bytes 1572880 | tf_op jit(solution)/shard_map/all_gather | solution.py:55
  707.8 2.7 copy.39
  (26 shorter events, 1.5 us)
Async XLA Ops:
  7.2 90.9 %all-gather.7.cloned.1.call-start = ((), (), s32[]{:S(2)}) async-start(), calls=%async_computation.3 | async-start | bytes 1671168 | tf_op jit(solution)/shard_map/all_gather | solution.py:36
  8.8 230.7 %all-gather.5.cloned.1.call-start = ((), (), s32[]{:S(2)}) async-start(), calls=%async_computation.2 | async-start | bytes 13369344 | tf_op jit(solution)/shard_map/all_gather | solution.py:37
  9.6 343.5 %reduce-scatter.7.cloned.1.call-start = ((), (), s32[]{:S(2)}) async-start(), calls=%async_computation.6 | async-start | bytes 3342336 | tf_op jit(solution)/shard_map/reduce_scatter | solution.py:45
  261.1 168.0 %copy-start = (f32[192,256]{1,0:T(8,128)S(1)}, f32[192,256]{1,0:T(8,128)}, u32[]{:S(2)}) copy-start(f32[192,256]{1,0:T(8,128)} %param.7) | copy-start | bytes 589828
  261.2 250.9 %all-gather.9.cloned.1.call-start = ((), (), s32[]{:S(2)}) async-start(), calls=%async_computation.4 | async-start | bytes 1671168 | tf_op jit(solution)/shard_map/all_gather | solution.py:49
  430.8 193.6 %reduce-scatter.9.cloned.1.call-start = ((), (), s32[]{:S(2)}) async-start(), calls=%async_computation.7 | async-start | bytes 3342336 | tf_op jit(solution)/shard_map/reduce_scatter | solution.py:50
  529.1 95.3 %copy-start.1 = (f32[192,256]{1,0:T(8,128)S(1)}, f32[192,256]{1,0:T(8,128)}, u32[]{:S(2)}) copy-start(f32[192,256]{1,0:T(8,128)} %param.8) | copy-start | bytes 589828
  529.1 95.3 %copy-start.2 = (f32[192,256]{1,0:T(8,128)S(1)}, f32[192,256]{1,0:T(8,128)}, u32[]{:S(2)}) copy-start(f32[192,256]{1,0:T(8,128)} %param.9) | copy-start | bytes 589828
  529.1 178.7 %all-gather.11.cloned.1.call-start = ((), (), s32[]{:S(2)}) async-start(), calls=%async_computation.5 | async-start | bytes 1671168 | tf_op jit(solution)/shard_map/all_gather | solution.py:55
Sparse Core Ops, SparseCore 0:
  10.4 87.6 all-gather.6
  100.8 138.6 all-gather.4
  261.3 91.7 reduce-scatter.6
  430.9 81.1 all-gather.8
  529.2 95.0 reduce-scatter.8
  626.6 81.2 all-gather.10
where the time goes:
time: 718 us; the launch traced here: 717 us
  waiting for transfers between devices  579 us (81%)
  blocking collectives  73.7 us (10%)
  matrix products  30 us (4%)
  between operations  14.9 us (2%)
  local copies, waits for them, and re-layouts  11.1 us (2%)
  other arithmetic  8.24 us (1%)
    all_gather x1, waiting for transfers between devices, on_device(): replica_rows = lax.all_gather(patches, 'shard', axis=0, tiled=True)  141 us
    reduce_scatter x1, waiting for transfers between devices, on_device(): lax.psum_scatter(local_grad(weight1), 'dp', scatter_dimension=0, tiled=True)  95.2 us
    reduce_scatter x1, waiting for transfers between devices, on_device(): grad1_part = lax.psum_scatter(grad1, 'dp', scatter_dimension=0, tiled=True)  91.9 us
    all_gather x1, waiting for transfers between devices, on_device(): weight0 = lax.all_gather(weight0_part, 'dp', axis=0, tiled=True)  87 us
    all_gather x1, waiting for transfers between devices, on_device(): lax.all_gather(new_master.astype(jnp.bfloat16), 'dp', axis=0, tiled=True)  81.6 us
    all_gather x1, waiting for transfers between devices, on_device(): weight1 = lax.all_gather(tilted_part, 'dp', axis=0, tiled=True)  81.1 us
    psum x1, blocking collectives, on_device(): total = lax.psum(jnp.sum(grad1_part * grad1_part), ('dp', 'shard'))  73.7 us
    dot_general x2, matrix products, contract_rows(): lax.dot_general(left, right, (((0,), (0,)), ((), ())), preferred_element_...  16.1 us
  transfers between devices with their start and end apart: 6, of which 6 were waited for; matrix products, arithmetic and copies ran while one was open for 0% of the time, Pallas kernels for 0%

commit v1 on v0

v1 whole, which is shorter than its diff:
```python
import jax
import jax.numpy as jnp
from jax import lax
from jax.experimental import pallas as pl
from jax.experimental.pallas import tpu as pltpu
from jax.sharding import PartitionSpec as P

D = 3072
HEAD = 128
QW = 4096
COLS = 256
REPLICA = 2048
BLOCK = 128
PART = 192
HALF = 96
PIECE = 768

MOMENT_FIX = 0.9999734386011124
SECOND_FIX = 0.994079470779666

MESH = pl.DeviceIdType.MESH
f32 = jnp.float32
bf16 = jnp.bfloat16


class Slots:
    def __init__(self):
        self.count = 0

    def take(self, *dims):
        start, size = self.count, 1
        for dim in dims:
            size *= dim
        self.count += size

        def at(*index):
            flat = 0
            for dim, i in zip(dims, index, strict=True):
                flat = flat * dim + i
            return start + flat

        return at


SLOTS = Slots()
Y_SEM = SLOTS.take(2, 2, 4)
YF_SEM = SLOTS.take(2, 2, 4)
Z4_SEM = SLOTS.take(4)
SIB_SEM = SLOTS.take(2, 7)
AG_Z, AG_X, AG_F = SLOTS.take(3, 4), SLOTS.take(3, 2, 4), SLOTS.take(3, 2, 4)
RS_F, RS_X, RS_Z = SLOTS.take(2, 2, 4), SLOTS.take(2, 2, 4), SLOTS.take(2, 4)
SUM_SEM = SLOTS.take(2, 16)
N_SEM = SLOTS.count


def norm_backward(query, centred_cot):
    parts = []
    for head in range(COLS // HEAD):
        lanes = slice(head * HEAD, (head + 1) * HEAD)
        x, c = query[:, lanes], centred_cot[:, lanes]
        x = x - jnp.sum(x, axis=1, keepdims=True) * (1.0 / HEAD)
        var = jnp.sum(x * x, axis=1, keepdims=True) * (1.0 / HEAD)
        rstd = 1.0 / jnp.sqrt(var + 1e-06)
        normed = x * rstd
        inner = jnp.sum(c * normed, axis=1, keepdims=True) * (1.0 / HEAD)
        parts.append((rstd * (c - normed * inner)).astype(bf16))
    return jnp.concatenate(parts, axis=1)


def kernel(
    patches, cot, master, moment, second,
    new_weight, new_master, new_moment, new_second,
    pat, cots, centred, w0, g1, w1, nw, dq,
    plus, minus, mine, b_two, b_plus, b_minus, b_z, r_f, r_x, r_z, sums, tile,
    ssem, rsem, lsem,
):
    dp, sh = lax.axis_index("dp"), lax.axis_index("shard")
    x, zl = dp // 4, dp % 4
    y = (sh // 2) % 4

    def at_x(step):
        return ((x + step) % 4) * 4 + zl, sh

    def at_z(step):
        return x * 4 + (zl + step) % 4, sh

    def at_y(step):
        return dp, (sh // 8) * 8 + ((y + step) % 4) * 2 + sh % 2

    far = (dp, (sh + 8) % 16)
    sibling = (dp, sh + 1 - 2 * (sh % 2))

    def copy(src, dst, slot, to):
        return pltpu.make_async_remote_copy(
            src_ref=src, dst_ref=dst, send_sem=ssem.at[slot], recv_sem=rsem.at[slot],
            device_id=to, device_id_type=MESH,
        )

    started = []

    def send(src, dst, slot, to):
        one = copy(src, dst, slot, to)
        one.start()
        started.append(one)

    def arrived(ref, slot):
        copy(ref, ref, slot, sibling).wait_recv()

    def rows(start, size, by):
        return pl.ds(pl.multiple_of(start, by), size)

    own = pat.at[rows(sh * BLOCK, BLOCK, BLOCK)]
    load = pltpu.make_async_copy(patches, own, lsem.at[0])
    load.start()
    load_cot = pltpu.make_async_copy(cot, cots, lsem.at[1])
    load_cot.start()
    barrier = pltpu.get_barrier_semaphore()

    @pl.loop(1, 16)
    def _(p):
        pl.semaphore_signal(barrier, inc=1, device_id=((dp + p) % 16, sh), device_id_type=MESH)
        pl.semaphore_signal(barrier, inc=1, device_id=(dp, (sh + p) % 16), device_id_type=MESH)

    w0[rows(dp * PART, PART, PART), :] = master[...].astype(bf16)
    load.wait()
    with jax.named_scope("entry"):
        pl.semaphore_wait(barrier, 30)

    def gather_start(k, buf):
        part = buf.at[rows(dp * PART, PART, PART)]
        for r in (1, 3, 2):
            send(part, part, AG_Z(k, r), at_z(r))
        send(part, part, AG_X(k, 0, 0), at_x(1))
        send(part, part, AG_X(k, 1, 0), at_x(3))

    def gather_z(k, buf):
        for r in (1, 3, 2):
            part = buf.at[rows((x * 4 + (zl + 4 - r) % 4) * PART, PART, PART)]
            arrived(part, AG_Z(k, r))
            send(part, part, AG_X(k, 0, r), at_x(1))
            send(part, part, AG_X(k, 1, r), at_x(3))

    def gather_x(k, buf):
        for r in (0, 1, 3, 2):
            zz = (zl + 4 - r) % 4
            low = ((x + 3) % 4 * 4 + zz) * PART
            arrived(buf.at[rows(low, PART, PART)], AG_X(k, 0, r))
            half = buf.at[rows(low, HALF, HALF)]
            send(half, half, AG_F(k, 0, r), at_x(1))
            high = ((x + 1) % 4 * 4 + zz) * PART
            arrived(buf.at[rows(high, PART, PART)], AG_X(k, 1, r))
            half = buf.at[rows(high + HALF, HALF, HALF)]
            send(half, half, AG_F(k, 1, r), at_x(3))

    def gather_end(k, buf):
        for r in (0, 1, 3, 2):
            start = ((x + 2) % 4 * 4 + (zl + 4 - r) % 4) * PART
            arrived(buf.at[rows(start, HALF, HALF)], AG_F(k, 0, r))
            arrived(buf.at[rows(start + HALF, HALF, HALF)], AG_F(k, 1, r))

    def home(half):
        return (sh + 8 * half) % 16

    def y_block(half, step):
        base = home(half)
        return ((base // 8) * 8 + ((y + step) % 4) * 2 + base % 2) * BLOCK

    def y_send(half, q):
        part = pat.at[rows(home(half) * BLOCK + q * 32, 32, 32)]
        send(part, part, Y_SEM(half, 0, q), at_y(1))
        send(part, part, Y_SEM(half, 1, q), at_y(3))

    def y_forward(half, q):
        low = y_block(half, 3) + q * 32
        arrived(pat.at[rows(low, 32, 32)], Y_SEM(half, 0, q))
        part = pat.at[rows(low, 16, 16)]
        send(part, part, YF_SEM(half, 0, q), at_y(1))
        high = y_block(half, 1) + q * 32
        arrived(pat.at[rows(high, 32, 32)], Y_SEM(half, 1, q))
        part = pat.at[rows(high + 16, 16, 16)]
        send(part, part, YF_SEM(half, 1, q), at_y(3))

    def y_last(half, q):
        start = y_block(half, 2) + q * 32
        arrived(pat.at[rows(start, 16, 16)], YF_SEM(half, 0, q))
        arrived(pat.at[rows(start + 16, 16, 16)], YF_SEM(half, 1, q))
        part = pat.at[rows(start, 32, 32)]
        send(part, part, SIB_SEM(half, 3 + q), sibling)

    def share(half, step, slot):
        part = pat.at[rows(y_block(half, step), BLOCK, BLOCK)]
        send(part, part, SIB_SEM(half, slot), sibling)

    def theirs(half, step):
        return y_block(half, step) // (2 * BLOCK) * (2 * BLOCK) + (1 - sh % 2) * BLOCK

    def shared(half, step, slot):
        arrived(pat.at[rows(theirs(half, step), BLOCK, BLOCK)], SIB_SEM(half, slot))

    def shared_last(half):
        for q in range(4):
            arrived(pat.at[rows(theirs(half, 2) + q * 32, 32, 32)], SIB_SEM(half, 3 + q))

    def block_of(half, step):
        part = rows(y_block(half, step) // (2 * BLOCK) * (2 * BLOCK), 2 * BLOCK, 2 * BLOCK)
        query = jnp.dot(pat[part, :], w0[...], preferred_element_type=f32)
        dq[part, :] = norm_backward(query, centred[part, :])

    for q in range(4):
        y_send(0, q)
    for q in range(4):
        part = pat.at[rows(sh * BLOCK + q * 32, 32, 32)]
        send(part, part, Z4_SEM(q), far)
    share(0, 0, 0)
    gather_start(0, w0)

    load_cot.wait()

    @pl.loop(0, 8)
    def _(i):
        part = rows(i * 256, 256, 256)
        for head in range(COLS // HEAD):
            lanes = slice(head * HEAD, (head + 1) * HEAD)
            c = cots[part, lanes].astype(f32)
            centred[part, lanes] = c - jnp.sum(c, axis=1, keepdims=True) * (1.0 / HEAD)

    def z4_pass(q):
        arrived(pat.at[rows(home(1) * BLOCK + q * 32, 32, 32)], Z4_SEM(q))
        y_send(1, q)

    with jax.named_scope("w0_z"):
        gather_z(0, w0)
    with jax.named_scope("y0"):
        for q in range(4):
            y_forward(0, q)
    share(0, 3, 1)
    share(0, 1, 2)
    with jax.named_scope("w0_x"):
        gather_x(0, w0)
        gather_end(0, w0)
    with jax.named_scope("z4a"):
        z4_pass(0)
        z4_pass(1)
    shared(0, 0, 0)
    block_of(0, 0)
    shared(0, 3, 1)
    block_of(0, 3)
    shared(0, 1, 2)
    block_of(0, 1)
    with jax.named_scope("y0_last"):
        for q in range(4):
            y_last(0, q)
    with jax.named_scope("z4b"):
        z4_pass(2)
        z4_pass(3)
    share(1, 0, 0)
    shared_last(0)
    block_of(0, 2)
    shared(1, 0, 0)
    block_of(1, 0)
    with jax.named_scope("y1"):
        for q in range(4):
            y_forward(1, q)
    share(1, 3, 1)
    share(1, 1, 2)
    with jax.named_scope("blocks"):
        shared(1, 3, 1)
        block_of(1, 3)
        shared(1, 1, 2)
        block_of(1, 1)
    with jax.named_scope("y1_last"):
        for q in range(4):
            y_last(1, q)
    shared_last(1)
    block_of(1, 2)

    def piece(step):
        lanes = pl.ds(pl.multiple_of((x + step) % 4 * PIECE, PIECE), PIECE)
        return lax.dot_general(
            pat[:, lanes], dq[...], (((0,), (0,)), ((), ())), preferred_element_type=f32
        )

    ORDER = (2, 1, 3, 0)

    def reduce_scatter(k):
        with jax.named_scope("rs_two"):
            b_two[...] = piece(2).astype(bf16)
        for r in ORDER:
            start = (zl + r) % 4 * PART
            send(b_two.at[rows(start, HALF, HALF)], r_f.at[k, 0, r], RS_F(k, 0, r), at_x(1))
            send(b_two.at[rows(start + HALF, HALF, HALF)], r_f.at[k, 1, r], RS_F(k, 1, r), at_x(3))
        with jax.named_scope("rs_pm"):
            plus[...] = piece(1)
            minus[...] = piece(3)
        with jax.named_scope("rs_x"):
            for r in ORDER:
                start = (zl + r) % 4 * PART
                low, high = rows(start, HALF, HALF), rows(start + HALF, HALF, HALF)
                both = rows(start, PART, PART)
                arrived(r_f.at[k, 0, r], RS_F(k, 0, r))
                b_plus[low, :] = (plus[low, :] + r_f[k, 0, r].astype(f32)).astype(bf16)
                b_plus[high, :] = plus[high, :].astype(bf16)
                send(b_plus.at[both], r_x.at[k, 0, r], RS_X(k, 0, r), at_x(1))
                arrived(r_f.at[k, 1, r], RS_F(k, 1, r))
                b_minus[low, :] = minus[low, :].astype(bf16)
                b_minus[high, :] = (minus[high, :] + r_f[k, 1, r].astype(f32)).astype(bf16)
                send(b_minus.at[both], r_x.at[k, 1, r], RS_X(k, 1, r), at_x(3))
                if r == ORDER[0]:
                    mine[...] = piece(0)
        with jax.named_scope("rs_z"):
            for r in ORDER:
                both = rows((zl + r) % 4 * PART, PART, PART)
                arrived(r_x.at[k, 0, r], RS_X(k, 0, r))
                arrived(r_x.at[k, 1, r], RS_X(k, 1, r))
                total = mine[both, :] + r_x[k, 0, r].astype(f32) + r_x[k, 1, r].astype(f32)
                if r:
                    b_z[k, r] = total.astype(bf16)
                    send(b_z.at[k, r], r_z.at[k, r], RS_Z(k, r), at_z(r))
        with jax.named_scope("rs_end"):
            for r in (2, 1, 3):
                arrived(r_z.at[k, r], RS_Z(k, r))
                total = total + r_z[k, r].astype(f32)
        return total

    def finish():
        for one in started:
            one.wait_send()
        started.clear()

    grad1 = reduce_scatter(0)
    finish()
    g1[rows(dp * PART, PART, PART), :] = grad1.astype(bf16)
    gather_start(1, g1)

    square = (grad1 * grad1).reshape(PART // 8, 8, COLS)
    square = jnp.sum(square, axis=0)
    tile[0] = square[:, :128] + square[:, 128:]

    def sum_copy(stage, p):
        to = ((dp + p) % 16, sh) if stage == 0 else (dp, (sh + p) % 16)
        return copy(tile.at[stage], sums.at[stage, p], SUM_SEM(stage, p), to)

    def sum_start(stage):
        @pl.loop(1, 16)
        def _(p):
            sum_copy(stage, p).start()

    def sum_end(stage):
        def add(p, total):
            sum_copy(stage, p).wait()
            return total + sums[stage, p]

        return lax.fori_loop(1, 16, add, tile[stage])

    sum_start(0)
    with jax.named_scope("g1_z"):
        gather_z(1, g1)
    with jax.named_scope("sum0"):
        tile[1] = sum_end(0)
    sum_start(1)
    with jax.named_scope("g1_x"):
        gather_x(1, g1)
    with jax.named_scope("sum1"):
        total = jnp.sum(sum_end(1))
    scale = jnp.sqrt(f32(D * QW)) / jnp.sqrt(total + 1e-12)
    with jax.named_scope("g1_end"):
        gather_end(1, g1)

    with jax.named_scope("pass2"):

        @pl.loop(0, 8)
        def _(i):
            part = rows(i * 384, 384, 384)
            w1[part, :] = (w0[part, :].astype(f32) + scale * g1[part, :].astype(f32)).astype(bf16)

        @pl.loop(0, 4)
        def _(i):
            part = rows(i * 512, 512, 512)
            query = jnp.dot(pat[part, :], w1[...], preferred_element_type=f32)
            dq[part, :] = norm_backward(query, centred[part, :])

    finish()
    grad2 = reduce_scatter(1)
    finish()
    weights = master[...]
    next_moment = 0.9 * moment[...] + 0.1 * grad2
    next_second = 0.95 * second[...] + 0.05 * grad2 * grad2
    update = next_moment / MOMENT_FIX / (jnp.sqrt(next_second / SECOND_FIX) + 1e-08) + 0.1 * weights
    next_master = weights - 0.05 * update
    nw[rows(dp * PART, PART, PART), :] = next_master.astype(bf16)
    gather_start(2, nw)
    new_master[...] = next_master
    new_moment[...] = next_moment
    new_second[...] = next_second
    with jax.named_scope("nw"):
        gather_z(2, nw)
        gather_x(2, nw)
        gather_end(2, nw)
    out = pltpu.make_async_copy(nw, new_weight, lsem.at[0])
    out.start()
    finish()
    out.wait()


def on_device(patches, cot, master, moment, second):
    state = jax.ShapeDtypeStruct((PART, COLS), f32)
    any_ref, vmem = pl.BlockSpec(memory_space=pl.ANY), pl.BlockSpec(memory_space=pltpu.VMEM)
    return pl.pallas_call(
        kernel,
        name="sam_step",
        out_shape=(jax.ShapeDtypeStruct((D, COLS), bf16), state, state, state),
        in_specs=[any_ref, any_ref, vmem, vmem, vmem],
        out_specs=(any_ref, vmem, vmem, vmem),
        scratch_shapes=[
            pltpu.VMEM((REPLICA, D), bf16),
            pltpu.VMEM((REPLICA, COLS), bf16),
            pltpu.VMEM((REPLICA, COLS), f32),
            pltpu.VMEM((D, COLS), bf16),
            pltpu.VMEM((D, COLS), bf16),
            pltpu.VMEM((D, COLS), bf16),
            pltpu.VMEM((D, COLS), bf16),
            pltpu.VMEM((REPLICA, COLS), bf16),
            pltpu.VMEM((PIECE, COLS), f32),
            pltpu.VMEM((PIECE, COLS), f32),
            pltpu.VMEM((PIECE, COLS), f32),
            pltpu.VMEM((PIECE, COLS), bf16),
            pltpu.VMEM((PIECE, COLS), bf16),
            pltpu.VMEM((PIECE, COLS), bf16),
            pltpu.VMEM((2, 4, PART, COLS), bf16),
            pltpu.VMEM((2, 2, 4, HALF, COLS), bf16),
            pltpu.VMEM((2, 2, 4, PART, COLS), bf16),
            pltpu.VMEM((2, 4, PART, COLS), bf16),
            pltpu.VMEM((2, 16, 8, 128), f32),
            pltpu.VMEM((2, 8, 128), f32),
            pltpu.SemaphoreType.DMA((N_SEM,)),
            pltpu.SemaphoreType.DMA((N_SEM,)),
            pltpu.SemaphoreType.DMA((2,)),
        ],
        compiler_params=pltpu.CompilerParams(
            collective_id=0, has_side_effects=True, vmem_limit_bytes=56 * 2**20
        ),
    )(patches, cot, master, moment, second)


def solution(mesh):
    in_specs = (
        P(("dp", "shard"), None),
        P("dp", "shard"),
        P("dp", "shard"),
        P("dp", "shard"),
        P("dp", "shard"),
    )
    out_specs = (P(None, "shard"), P("dp", "shard"), P("dp", "shard"), P("dp", "shard"))
    return jax.shard_map(
        on_device, mesh=mesh, in_specs=in_specs, out_specs=out_specs, check_vma=False
    )
```

time: 718 us -> 187 us (0.26)
  waiting for transfers between devices: 579 us -> 0 us
  Pallas kernels: 0 us -> 181 us
  blocking collectives: 73.7 us -> 0 us
  matrix products: 30 us -> 0 us
  between operations: 14.9 us -> 0.67 us
  other arithmetic: 8.24 us -> 0 us
    all_gather x4 -> x0, waiting for transfers between devices: 391 us -> none  [the longest x1 141 us: on_device(): replica_rows = lax.all_gather(patches, 'shard', axis=0, tiled=True)]
    reduce_scatter x2 -> x0, waiting for transfers between devices: 187 us -> none  [the longest x1 95.2 us: on_device(): lax.psum_scatter(local_grad(weight1), 'dp', scatter_dimension=0, tiled=True)]
    pallas_call x0 -> x1, Pallas kernels: none -> 181 us  [on_device(): pl.pallas_call(kernel, name='sam_step', out_shape=(jax.ShapeDtypeStruct((...]
    psum x1 -> x0, blocking collectives: 73.7 us -> none  [on_device(): total = lax.psum(jnp.sum(grad1_part * grad1_part), ('dp', 'shard'))]
    dot_general x4 -> x0, matrix products: 30 us -> none  [the longest x2 16.1 us: contract_rows(): lax.dot_general(left, right, (((0,), (0,)), ((), ())), preferred_element_...]
  transfers between devices with their start and end apart: 6 -> 0, of which waited for: 6 -> 0; matrix products, arithmetic and copies ran while one was open for 0% -> 0% of each run, Pallas kernels for 0% -> 0%
where the time goes in v1:
time: 187 us
  Pallas kernels  181 us (97%)
  local copies, waits for them, and re-layouts  4.75 us (3%)
    pallas_call x1, Pallas kernels, on_device(): pl.pallas_call(kernel, name='sam_step', out_shape=(jax.ShapeDtypeStruct((...  181 us
    unnamed x10, local copies, waits for them, and re-layouts  4.75 us

profile of v1, /device:TPU:8, one launch (start us, length us, event | category | flops | bytes accessed | tf_op | source)
XLA Modules:
  0.0 186.8 jit_solution(15142718578366532414)
XLA Ops:
  0.6 181.4 %sam_step.1 = (bf16[3072,256]{1,0:T(8,128)(2,1)}, f32[192,256]{1,0:T(8,128)}, f32[192,256]{1,0:T(8,128)}, f32[192,256]{1,0:T(8,128)}) custom-call(bf16[128,3072]{1,0:T(8,128)(2,1)} %patches.1, bf16[2048,256]{1,0:T(8,128)(2,1)} %cot.1, f32[192,256]{1,0:T(8,128)} %master.1, f32[192,256]{1,0:T(8,128)} %moment.1, f32[192,256]{1,0:T(8,128)} %second.1), custom_call_target="tpu_custom_call" | custom-call | tf_op jit(solution)/shard_map/sam_step/pallas_call | solution.py:408
  182.1 0.0 copy-start.2
  182.1 0.0 copy-start.1
  182.1 0.0 copy-start
  182.1 2.7 %copy.13 = bf16[3072,256]{1,0:T(8,128)(2,1)} copy(bf16[3072,256]{1,0:T(8,128)(2,1)} %get-tuple-element.8) | data formatting | bytes 3145728
  184.8 0.0 copy-done.2
  184.8 0.7 copy.14
  185.5 0.0 copy-done.1
  185.5 0.7 copy.15
  186.2 0.0 copy-done
  186.2 0.7 copy.16
Async XLA Ops:
  182.1 2.7 %copy-start.2 = (f32[192,256]{1,0:T(8,128)S(1)}, f32[192,256]{1,0:T(8,128)}, u32[]{:S(2)}) copy-start(f32[192,256]{1,0:T(8,128)} %get-tuple-element.9) | copy-start | bytes 589828
  182.1 3.4 %copy-start.1 = (f32[192,256]{1,0:T(8,128)S(1)}, f32[192,256]{1,0:T(8,128)}, u32[]{:S(2)}) copy-start(f32[192,256]{1,0:T(8,128)} %get-tuple-element.10) | copy-start | bytes 589828
  182.1 4.1 %copy-start = (f32[192,256]{1,0:T(8,128)S(1)}, f32[192,256]{1,0:T(8,128)}, u32[]{:S(2)}) copy-start(f32[192,256]{1,0:T(8,128)} %get-tuple-element.11) | copy-start | bytes 589828

commit v2 on v1

v2 whole, which is shorter than its diff:
```python
import jax
import jax.numpy as jnp
from jax import lax
from jax.experimental import pallas as pl
from jax.experimental.pallas import tpu as pltpu
from jax.sharding import PartitionSpec as P

D = 3072
HEAD = 128
QW = 4096
COLS = 256
REPLICA = 2048
BLOCK = 128
PART = 192
PIECE = 768
CUTS = 2
SUB = PART // CUTS
HALF = SUB // 2

MOMENT_FIX = 0.9999734386011124
SECOND_FIX = 0.994079470779666

MESH = pl.DeviceIdType.MESH
f32 = jnp.float32
bf16 = jnp.bfloat16


class Slots:
    def __init__(self):
        self.count = 0

    def take(self, *dims):
        start, size = self.count, 1
        for dim in dims:
            size *= dim
        self.count += size

        def at(*index):
            flat = 0
            for dim, i in zip(dims, index, strict=True):
                flat = flat * dim + i
            return start + flat

        return at


SLOTS = Slots()
Y_SEM = SLOTS.take(2, 2, 4)
YF_SEM = SLOTS.take(2, 2, 4)
Z4_SEM = SLOTS.take(4)
SIB_SEM = SLOTS.take(2, 7)
AG_Z, AG_X, AG_F = SLOTS.take(3, CUTS, 4), SLOTS.take(3, CUTS, 2, 4), SLOTS.take(3, CUTS, 2, 4)
RS_F, RS_X, RS_Z = SLOTS.take(2, CUTS, 2, 4), SLOTS.take(2, CUTS, 2, 4), SLOTS.take(2, CUTS, 4)
SUM_SEM = SLOTS.take(2, 16)
N_SEM = SLOTS.count


def norm_backward(query, centred_cot):
    parts = []
    for head in range(COLS // HEAD):
        lanes = slice(head * HEAD, (head + 1) * HEAD)
        x, c = query[:, lanes], centred_cot[:, lanes]
        x = x - jnp.sum(x, axis=1, keepdims=True) * (1.0 / HEAD)
        var = jnp.sum(x * x, axis=1, keepdims=True) * (1.0 / HEAD)
        rstd = 1.0 / jnp.sqrt(var + 1e-06)
        normed = x * rstd
        inner = jnp.sum(c * normed, axis=1, keepdims=True) * (1.0 / HEAD)
        parts.append((rstd * (c - normed * inner)).astype(bf16))
    return jnp.concatenate(parts, axis=1)


def kernel(
    patches, cot, master_in, moment_in, second_in,
    new_weight, new_master, new_moment, new_second,
    master, moment, second, pat, cots, centred, w0, g1, w1, nw, dq,
    plus, minus, mine, b_two, b_plus, b_minus, b_z, r_f, r_x, r_z, sums, tile, query,
    ssem, rsem, lsem,
):
    dp, sh = lax.axis_index("dp"), lax.axis_index("shard")
    x, zl = dp // 4, dp % 4
    y = (sh // 2) % 4

    def at_x(step):
        return ((x + step) % 4) * 4 + zl, sh

    def at_z(step):
        return x * 4 + (zl + step) % 4, sh

    def at_y(step):
        return dp, (sh // 8) * 8 + ((y + step) % 4) * 2 + sh % 2

    far = (dp, (sh + 8) % 16)
    sibling = (dp, sh + 1 - 2 * (sh % 2))

    def copy(src, dst, slot, to):
        return pltpu.make_async_remote_copy(
            src_ref=src, dst_ref=dst, send_sem=ssem.at[slot], recv_sem=rsem.at[slot],
            device_id=to, device_id_type=MESH,
        )

    started = []

    def send(src, dst, slot, to):
        one = copy(src, dst, slot, to)
        one.start()
        started.append(one)

    def finish():
        for one in started:
            one.wait_send()
        started.clear()

    def arrived(ref, slot):
        copy(ref, ref, slot, sibling).wait_recv()

    def rows(start, size, by):
        return pl.ds(pl.multiple_of(start, by), size)

    barrier = pltpu.get_barrier_semaphore()

    @pl.loop(1, 16)
    def _(p):
        pl.semaphore_signal(barrier, inc=1, device_id=(dp, (sh + p) % 16), device_id_type=MESH)
        pl.semaphore_signal(barrier, inc=1, device_id=((dp + p) % 16, sh), device_id_type=MESH)

    own = pat.at[rows(sh * BLOCK, BLOCK, BLOCK)]
    loads = [
        pltpu.make_async_copy(src, dst, lsem.at[i])
        for i, (src, dst) in enumerate(
            ((master_in, master), (patches, own), (cot, cots), (moment_in, moment), (second_in, second))
        )
    ]
    for load in loads:
        load.start()
    loads[0].wait()
    w0[rows(dp * PART, PART, PART), :] = master[...].astype(bf16)
    loads[1].wait()
    with jax.named_scope("entry"):
        pl.semaphore_wait(barrier, 30)

    def gather_start(k, buf, h):
        part = buf.at[rows(dp * PART + h * SUB, SUB, SUB)]
        for r in (2, 1, 3):
            send(part, part, AG_Z(k, h, r), at_z(r))
        send(part, part, AG_X(k, h, 0, 0), at_x(1))
        send(part, part, AG_X(k, h, 1, 0), at_x(3))

    def gather_z(k, buf, h):
        for r in (1, 3, 2):
            part = buf.at[rows((x * 4 + (zl + 4 - r) % 4) * PART + h * SUB, SUB, SUB)]
            arrived(part, AG_Z(k, h, r))
            send(part, part, AG_X(k, h, 0, r), at_x(1))
            send(part, part, AG_X(k, h, 1, r), at_x(3))

    def gather_x(k, buf, h):
        for r in (0, 1, 3, 2):
            zz = (zl + 4 - r) % 4
            low = ((x + 3) % 4 * 4 + zz) * PART + h * SUB
            arrived(buf.at[rows(low, SUB, SUB)], AG_X(k, h, 0, r))
            half = buf.at[rows(low, HALF, HALF)]
            send(half, half, AG_F(k, h, 0, r), at_x(1))
            high = ((x + 1) % 4 * 4 + zz) * PART + h * SUB
            arrived(buf.at[rows(high, SUB, SUB)], AG_X(k, h, 1, r))
            half = buf.at[rows(high + HALF, HALF, HALF)]
            send(half, half, AG_F(k, h, 1, r), at_x(3))

    def gather_end(k, buf, h):
        for r in (0, 1, 3, 2):
            start = ((x + 2) % 4 * 4 + (zl + 4 - r) % 4) * PART + h * SUB
            arrived(buf.at[rows(start, HALF, HALF)], AG_F(k, h, 0, r))
            arrived(buf.at[rows(start + HALF, HALF, HALF)], AG_F(k, h, 1, r))

    def home(half):
        return (sh + 8 * half) % 16

    def y_block(half, step):
        base = home(half)
        return ((base // 8) * 8 + ((y + step) % 4) * 2 + base % 2) * BLOCK

    def y_send(half, q):
        part = pat.at[rows(home(half) * BLOCK + q * 32, 32, 32)]
        send(part, part, Y_SEM(half, 0, q), at_y(1))
        send(part, part, Y_SEM(half, 1, q), at_y(3))

    def y_forward(half, q):
        low = y_block(half, 3) + q * 32
        arrived(pat.at[rows(low, 32, 32)], Y_SEM(half, 0, q))
        part = pat.at[rows(low, 16, 16)]
        send(part, part, YF_SEM(half, 0, q), at_y(1))
        high = y_block(half, 1) + q * 32
        arrived(pat.at[rows(high, 32, 32)], Y_SEM(half, 1, q))
        part = pat.at[rows(high + 16, 16, 16)]
        send(part, part, YF_SEM(half, 1, q), at_y(3))

    def y_last(half, q):
        start = y_block(half, 2) + q * 32
        arrived(pat.at[rows(start, 16, 16)], YF_SEM(half, 0, q))
        arrived(pat.at[rows(start + 16, 16, 16)], YF_SEM(half, 1, q))
        part = pat.at[rows(start, 32, 32)]
        send(part, part, SIB_SEM(half, 3 + q), sibling)

    def share(half, step, slot):
        part = pat.at[rows(y_block(half, step), BLOCK, BLOCK)]
        send(part, part, SIB_SEM(half, slot), sibling)

    def theirs(half, step):
        return y_block(half, step) // (2 * BLOCK) * (2 * BLOCK) + (1 - sh % 2) * BLOCK

    def shared(half, step, slot):
        arrived(pat.at[rows(theirs(half, step), BLOCK, BLOCK)], SIB_SEM(half, slot))

    def shared_last(half):
        for q in range(4):
            arrived(pat.at[rows(theirs(half, 2) + q * 32, 32, 32)], SIB_SEM(half, 3 + q))

    def block_of(half, step):
        part = rows(y_block(half, step) // (2 * BLOCK) * (2 * BLOCK), 2 * BLOCK, 2 * BLOCK)
        query = jnp.dot(pat[part, :], w0[...], preferred_element_type=f32)
        dq[part, :] = norm_backward(query, centred[part, :])

    for h in range(CUTS):
        gather_start(0, w0, h)
    for q in range(4):
        y_send(0, q)
    share(0, 0, 0)

    loads[2].wait()

    @pl.loop(0, 8)
    def _(i):
        part = rows(i * 256, 256, 256)
        for head in range(COLS // HEAD):
            lanes = slice(head * HEAD, (head + 1) * HEAD)
            c = cots[part, lanes].astype(f32)
            centred[part, lanes] = c - jnp.sum(c, axis=1, keepdims=True) * (1.0 / HEAD)

    def z4_pass(q):
        arrived(pat.at[rows(home(1) * BLOCK + q * 32, 32, 32)], Z4_SEM(q))
        y_send(1, q)

    y_forward(0, 0)
    for h in range(CUTS):
        gather_z(0, w0, h)
    for q in range(4):
        part = pat.at[rows(sh * BLOCK + q * 32, 32, 32)]
        send(part, part, Z4_SEM(q), far)
    y_forward(0, 1)
    y_forward(0, 2)
    y_forward(0, 3)
    share(0, 3, 1)
    share(0, 1, 2)
    for h in range(CUTS):
        gather_x(0, w0, h)
    z4_pass(0)
    for h in range(CUTS):
        gather_end(0, w0, h)
    shared(0, 0, 0)
    block_of(0, 0)
    shared(0, 3, 1)
    block_of(0, 3)
    shared(0, 1, 2)
    block_of(0, 1)
    for q in range(4):
        y_last(0, q)
    z4_pass(1)
    shared_last(0)
    block_of(0, 2)
    y_forward(1, 0)
    z4_pass(2)
    y_forward(1, 1)
    z4_pass(3)
    share(1, 0, 0)
    y_forward(1, 2)
    shared(1, 0, 0)
    block_of(1, 0)
    y_forward(1, 3)
    share(1, 3, 1)
    share(1, 1, 2)
    for q in range(3):
        y_last(1, q)
    shared(1, 3, 1)
    block_of(1, 3)
    shared(1, 1, 2)
    block_of(1, 1)
    y_last(1, 3)
    shared_last(1)
    block_of(1, 2)

    def piece(step):
        lanes = pl.ds(pl.multiple_of((x + step) % 4 * PIECE, PIECE), PIECE)
        return lax.dot_general(
            pat[:, lanes], dq[...], (((0,), (0,)), ((), ())), preferred_element_type=f32
        )

    ORDER = (2, 1, 3, 0)

    def scatter_two(k, h):
        for r in ORDER:
            start = (zl + r) % 4 * PART + h * SUB
            send(b_two.at[rows(start, HALF, HALF)], r_f.at[k, h, 0, r], RS_F(k, h, 0, r), at_x(1))
            send(b_two.at[rows(start + HALF, HALF, HALF)], r_f.at[k, h, 1, r], RS_F(k, h, 1, r), at_x(3))

    def scatter_x(k, h):
        for r in ORDER:
            start = (zl + r) % 4 * PART + h * SUB
            low, high = rows(start, HALF, HALF), rows(start + HALF, HALF, HALF)
            both = rows(start, SUB, SUB)
            arrived(r_f.at[k, h, 0, r], RS_F(k, h, 0, r))
            b_plus[low, :] = (plus[low, :] + r_f[k, h, 0, r].astype(f32)).astype(bf16)
            b_plus[high, :] = plus[high, :].astype(bf16)
            send(b_plus.at[both], r_x.at[k, h, 0, r], RS_X(k, h, 0, r), at_x(1))
            arrived(r_f.at[k, h, 1, r], RS_F(k, h, 1, r))
            b_minus[low, :] = minus[low, :].astype(bf16)
            b_minus[high, :] = (minus[high, :] + r_f[k, h, 1, r].astype(f32)).astype(bf16)
            send(b_minus.at[both], r_x.at[k, h, 1, r], RS_X(k, h, 1, r), at_x(3))

    def scatter_z(k, h):
        for r in ORDER:
            both = rows((zl + r) % 4 * PART + h * SUB, SUB, SUB)
            arrived(r_x.at[k, h, 0, r], RS_X(k, h, 0, r))
            arrived(r_x.at[k, h, 1, r], RS_X(k, h, 1, r))
            total = mine[both, :] + r_x[k, h, 0, r].astype(f32) + r_x[k, h, 1, r].astype(f32)
            if r:
                b_z[k, h, r] = total.astype(bf16)
                send(b_z.at[k, h, r], r_z.at[k, h, r], RS_Z(k, h, r), at_z(r))
        mine[rows(zl * PART + h * SUB, SUB, SUB), :] = total

    def scatter_end(k, h):
        total = mine[rows(zl * PART + h * SUB, SUB, SUB), :]
        for r in (2, 1, 3):
            arrived(r_z.at[k, h, r], RS_Z(k, h, r))
            total = total + r_z[k, h, r].astype(f32)
        return total

    def scatter_start(k):
        b_two[...] = piece(2).astype(bf16)
        for h in range(CUTS):
            scatter_two(k, h)
        plus[...] = piece(1)
        minus[...] = piece(3)
        scatter_x(k, 0)
        mine[...] = piece(0)
        for h in range(1, CUTS):
            scatter_x(k, h)

    def squares(part):
        part = jnp.sum((part * part).reshape(SUB // 8, 8, COLS), axis=0)
        return part[:, :128] + part[:, 128:]

    scatter_start(0)
    square = None
    for h in range(CUTS):
        scatter_z(0, h)
        if h:
            gather_z(1, g1, h - 1)
        grad1 = scatter_end(0, h)
        g1[rows(dp * PART + h * SUB, SUB, SUB), :] = grad1.astype(bf16)
        gather_start(1, g1, h)
        square = squares(grad1) if square is None else square + squares(grad1)

    tile[0] = square

    def sum_copy(stage, p):
        to = ((dp + p) % 16, sh) if stage == 0 else (dp, (sh + p) % 16)
        return copy(tile.at[stage], sums.at[stage, p], SUM_SEM(stage, p), to)

    def sum_start(stage):
        @pl.loop(1, 16)
        def _(p):
            sum_copy(stage, p).start()

    def sum_end(stage):
        def add(p, total):
            sum_copy(stage, p).wait()
            return total + sums[stage, p]

        return lax.fori_loop(1, 16, add, tile[stage])

    earlier = list(started)
    started.clear()
    sum_start(0)
    for h in range(CUTS - 1):
        gather_x(1, g1, h)
    gather_z(1, g1, CUTS - 1)
    tile[1] = sum_end(0)
    sum_start(1)
    gather_x(1, g1, CUTS - 1)
    for one in earlier:
        one.wait_send()
    total = jnp.sum(sum_end(1))
    scale = jnp.sqrt(f32(D * QW)) / jnp.sqrt(total + 1e-12)

    def depth(step):
        return (x + step) % 4 * PIECE

    def tilt(step):
        part = rows(depth(step), PIECE, PIECE)
        w1[part, :] = (w0[part, :].astype(f32) + scale * g1[part, :].astype(f32)).astype(bf16)

    def share_of(part, step):
        span = rows(depth(step), PIECE, PIECE)
        return jnp.dot(pat[part, span], w1[span, :], preferred_element_type=f32)

    for step in (0, 1, 3):
        tilt(step)

    @pl.loop(0, 4)
    def _(i):
        part = rows(i * 512, 512, 512)
        query[part, :] = share_of(part, 0) + share_of(part, 1) + share_of(part, 3)

    for h in range(CUTS):
        gather_end(1, g1, h)
    tilt(2)

    @pl.loop(0, 4)
    def _(i):
        part = rows(i * 512, 512, 512)
        dq[part, :] = norm_backward(query[part, :] + share_of(part, 2), centred[part, :])


    scatter_start(1)
    for load in loads[3:]:
        load.wait()
    for h in range(CUTS):
        part = pl.ds(h * SUB, SUB)
        scatter_z(1, h)
        if h:
            gather_z(2, nw, h - 1)
        grad2 = scatter_end(1, h)
        weights = master[part, :]
        next_moment = 0.9 * moment[part, :] + 0.1 * grad2
        next_second = 0.95 * second[part, :] + 0.05 * grad2 * grad2
        update = next_moment / MOMENT_FIX / (jnp.sqrt(next_second / SECOND_FIX) + 1e-08) + 0.1 * weights
        next_master = weights - 0.05 * update
        nw[rows(dp * PART + h * SUB, SUB, SUB), :] = next_master.astype(bf16)
        gather_start(2, nw, h)
        new_master[part, :] = next_master
        new_moment[part, :] = next_moment
        new_second[part, :] = next_second
    for h in range(CUTS - 1):
        gather_x(2, nw, h)
    gather_z(2, nw, CUTS - 1)
    gather_x(2, nw, CUTS - 1)

    def place(step):
        part = rows(depth(step), PIECE, PIECE)
        new_weight[part, :] = nw[part, :]

    for step in (0, 1, 3):
        place(step)
    for h in range(CUTS):
        gather_end(2, nw, h)
    place(2)
    finish()


def on_device(patches, cot, master, moment, second):
    state = pltpu.VMEM((PART, COLS), f32)
    any_ref, vmem = pl.BlockSpec(memory_space=pl.ANY), pl.BlockSpec(memory_space=pltpu.VMEM)
    return pl.pallas_call(
        kernel,
        name="sam_step",
        out_shape=(pltpu.VMEM((D, COLS), bf16), state, state, state),
        in_specs=[any_ref] * 5,
        out_specs=(vmem, vmem, vmem, vmem),
        scratch_shapes=[
            pltpu.VMEM((PART, COLS), f32),
            pltpu.VMEM((PART, COLS), f32),
            pltpu.VMEM((PART, COLS), f32),
            pltpu.VMEM((REPLICA, D), bf16),
            pltpu.VMEM((REPLICA, COLS), bf16),
            pltpu.VMEM((REPLICA, COLS), f32),
            pltpu.VMEM((D, COLS), bf16),
            pltpu.VMEM((D, COLS), bf16),
            pltpu.VMEM((D, COLS), bf16),
            pltpu.VMEM((D, COLS), bf16),
            pltpu.VMEM((REPLICA, COLS), bf16),
            pltpu.VMEM((PIECE, COLS), f32),
            pltpu.VMEM((PIECE, COLS), f32),
            pltpu.VMEM((PIECE, COLS), f32),
            pltpu.VMEM((PIECE, COLS), bf16),
            pltpu.VMEM((PIECE, COLS), bf16),
            pltpu.VMEM((PIECE, COLS), bf16),
            pltpu.VMEM((2, CUTS, 4, SUB, COLS), bf16),
            pltpu.VMEM((2, CUTS, 2, 4, HALF, COLS), bf16),
            pltpu.VMEM((2, CUTS, 2, 4, SUB, COLS), bf16),
            pltpu.VMEM((2, CUTS, 4, SUB, COLS), bf16),
            pltpu.VMEM((2, 16, 8, 128), f32),
            pltpu.VMEM((2, 8, 128), f32),
            pltpu.VMEM((REPLICA, COLS), f32),
            pltpu.SemaphoreType.DMA((N_SEM,)),
            pltpu.SemaphoreType.DMA((N_SEM,)),
            pltpu.SemaphoreType.DMA((5,)),
        ],
        compiler_params=pltpu.CompilerParams(
            collective_id=0, has_side_effects=True, vmem_limit_bytes=56 * 2**20
        ),
    )(patches, cot, master, moment, second)


def solution(mesh):
    in_specs = (
        P(("dp", "shard"), None),
        P("dp", "shard"),
        P("dp", "shard"),
        P("dp", "shard"),
        P("dp", "shard"),
    )
    out_specs = (P(None, "shard"), P("dp", "shard"), P("dp", "shard"), P("dp", "shard"))
    return jax.shard_map(
        on_device, mesh=mesh, in_specs=in_specs, out_specs=out_specs, check_vma=False
    )
```

time: 187 us -> 169 us (0.904)
  Pallas kernels: 181 us -> 165 us
    pallas_call x1, Pallas kernels: 181 us -> 165 us  [on_device(): pl.pallas_call(kernel, name='sam_step', out_shape=(pltpu.VMEM((D, COLS),...]
    unnamed x10 -> x4, local copies, waits for them, and re-layouts: 4.75 us -> 3.17 us
where the time goes in v2:
time: 169 us
  Pallas kernels  165 us (98%)
  local copies, waits for them, and re-layouts  3.17 us (2%)
    pallas_call x1, Pallas kernels, on_device(): pl.pallas_call(kernel, name='sam_step', out_shape=(pltpu.VMEM((D, COLS),...  165 us

profile of v2, /device:TPU:8, one launch (start us, length us, event | category | flops | bytes accessed | tf_op | source)
XLA Modules:
  0.0 168.7 jit_solution(12157521006952729381)
XLA Ops:
  0.6 164.9 %sam_step.1 = (bf16[3072,256]{1,0:T(8,128)(2,1)S(1)}, f32[192,256]{1,0:T(8,128)S(1)}, f32[192,256]{1,0:T(8,128)S(1)}, f32[192,256]{1,0:T(8,128)S(1)}) custom-call(bf16[128,3072]{1,0:T(8,128)(2,1)} %patches.1, bf16[2048,256]{1,0:T(8,128)(2,1)} %cot.1, f32[192,256]{1,0:T(8,128)} %master_in.1, f32[192,256]{1,0:T(8,128)} %moment_in.1, f32[192,256]{1,0:T(8,128)} %second_in.1), custom_call_target="tpu_custom_call" | custom-call | tf_op jit(solution)/shard_map/sam_step/pallas_call | solution.py:461
  165.5 1.1 copy.13
  166.7 0.7 copy.14
  167.3 0.7 copy.15
  168.0 0.7 copy.16

commit v3 on v2

--- a/solution.py
+++ b/solution.py
@@ -72,8 +72,8 @@
 def kernel(
     patches, cot, master_in, moment_in, second_in,
     new_weight, new_master, new_moment, new_second,
-    master, moment, second, pat, cots, centred, w0, g1, w1, nw, dq,
-    plus, minus, mine, b_two, b_plus, b_minus, b_z, r_f, r_x, r_z, sums, tile, query,
+    master, moment, second, pat, cots, centred, w0, g1, nw, dq,
+    plus, minus, mine, b_two, b_plus, b_minus, b_z, r_f, r_x, r_z, sums, tile, query, lift,
     ssem, rsem, lsem,
 ):
     dp, sh = lax.axis_index("dp"), lax.axis_index("shard")
@@ -215,8 +215,9 @@
 
     def block_of(half, step):
         part = rows(y_block(half, step) // (2 * BLOCK) * (2 * BLOCK), 2 * BLOCK, 2 * BLOCK)
-        query = jnp.dot(pat[part, :], w0[...], preferred_element_type=f32)
-        dq[part, :] = norm_backward(query, centred[part, :])
+        first = jnp.dot(pat[part, :], w0[...], preferred_element_type=f32)
+        query[part, :] = first
+        dq[part, :] = norm_backward(first, centred[part, :])
 
     for h in range(CUTS):
         gather_start(0, w0, h)
@@ -387,37 +388,29 @@
     gather_x(1, g1, CUTS - 1)
     for one in earlier:
         one.wait_send()
-    total = jnp.sum(sum_end(1))
-    scale = jnp.sqrt(f32(D * QW)) / jnp.sqrt(total + 1e-12)
 
     def depth(step):
         return (x + step) % 4 * PIECE
 
-    def tilt(step):
-        part = rows(depth(step), PIECE, PIECE)
-        w1[part, :] = (w0[part, :].astype(f32) + scale * g1[part, :].astype(f32)).astype(bf16)
-
     def share_of(part, step):
         span = rows(depth(step), PIECE, PIECE)
-        return jnp.dot(pat[part, span], w1[span, :], preferred_element_type=f32)
-
-    for step in (0, 1, 3):
-        tilt(step)
+        return jnp.dot(pat[part, span], g1[span, :], preferred_element_type=f32)
 
     @pl.loop(0, 4)
     def _(i):
         part = rows(i * 512, 512, 512)
-        query[part, :] = share_of(part, 0) + share_of(part, 1) + share_of(part, 3)
+        lift[part, :] = share_of(part, 0) + share_of(part, 1) + share_of(part, 3)
 
     for h in range(CUTS):
         gather_end(1, g1, h)
-    tilt(2)
+    total = jnp.sum(sum_end(1))
+    scale = jnp.sqrt(f32(D * QW)) / jnp.sqrt(total + 1e-12)
 
     @pl.loop(0, 4)
     def _(i):
         part = rows(i * 512, 512, 512)
-        dq[part, :] = norm_backward(query[part, :] + share_of(part, 2), centred[part, :])
-
+        tilted = query[part, :] + scale * (lift[part, :] + share_of(part, 2))
+        dq[part, :] = norm_backward(tilted, centred[part, :])
 
     scatter_start(1)
     for load in loads[3:]:
@@ -474,7 +467,6 @@
             pltpu.VMEM((D, COLS), bf16),
             pltpu.VMEM((D, COLS), bf16),
             pltpu.VMEM((D, COLS), bf16),
-            pltpu.VMEM((D, COLS), bf16),
             pltpu.VMEM((REPLICA, COLS), bf16),
             pltpu.VMEM((PIECE, COLS), f32),
             pltpu.VMEM((PIECE, COLS), f32),
@@ -489,6 +481,7 @@
             pltpu.VMEM((2, 16, 8, 128), f32),
             pltpu.VMEM((2, 8, 128), f32),
             pltpu.VMEM((REPLICA, COLS), f32),
+            pltpu.VMEM((REPLICA, COLS), f32),
             pltpu.SemaphoreType.DMA((N_SEM,)),
             pltpu.SemaphoreType.DMA((N_SEM,)),
             pltpu.SemaphoreType.DMA((5,)),

time: 169 us -> 165 us (0.976)
  Pallas kernels: 165 us -> 161 us
    pallas_call x1, Pallas kernels: 165 us -> 161 us  [on_device(): pl.pallas_call(kernel, name='sam_step', out_shape=(pltpu.VMEM((D, COLS),...]
where the time goes in v3:
time: 165 us; the launch traced here: 164 us
  Pallas kernels  161 us (98%)
  local copies, waits for them, and re-layouts  3.17 us (2%)
    pallas_call x1, Pallas kernels, on_device(): pl.pallas_call(kernel, name='sam_step', out_shape=(pltpu.VMEM((D, COLS),...  161 us

profile of v3, /device:TPU:8, one launch (start us, length us, event | category | flops | bytes accessed | tf_op | source)
XLA Modules:
  0.0 164.3 jit_solution(5194281828027900821)
XLA Ops:
  0.6 160.5 %sam_step.1 = (bf16[3072,256]{1,0:T(8,128)(2,1)S(1)}, f32[192,256]{1,0:T(8,128)S(1)}, f32[192,256]{1,0:T(8,128)S(1)}, f32[192,256]{1,0:T(8,128)S(1)}) custom-call(bf16[128,3072]{1,0:T(8,128)(2,1)} %patches.1, bf16[2048,256]{1,0:T(8,128)(2,1)} %cot.1, f32[192,256]{1,0:T(8,128)} %master_in.1, f32[192,256]{1,0:T(8,128)} %moment_in.1, f32[192,256]{1,0:T(8,128)} %second_in.1), custom_call_target="tpu_custom_call" | custom-call | tf_op jit(solution)/shard_map/sam_step/pallas_call | solution.py:454
  161.1 1.1 copy.13
  162.3 0.7 copy.14
  163.0 0.7 copy.15
  163.6 0.7 copy.16

commit v4 on v3

--- a/solution.py
+++ b/solution.py
@@ -73,7 +73,7 @@
     patches, cot, master_in, moment_in, second_in,
     new_weight, new_master, new_moment, new_second,
     master, moment, second, pat, cots, centred, w0, g1, nw, dq,
-    plus, minus, mine, b_two, b_plus, b_minus, b_z, r_f, r_x, r_z, sums, tile, query, lift,
+    two, plus, minus, mine, b_two, b_plus, b_minus, b_z, r_f, r_x, r_z, sums, tile, query, lift,
     ssem, rsem, lsem,
 ):
     dp, sh = lax.axis_index("dp"), lax.axis_index("shard")
@@ -140,7 +140,7 @@
 
     def gather_start(k, buf, h):
         part = buf.at[rows(dp * PART + h * SUB, SUB, SUB)]
-        for r in (2, 1, 3):
+        for r in (2, 3, 1):
             send(part, part, AG_Z(k, h, r), at_z(r))
         send(part, part, AG_X(k, h, 0, 0), at_x(1))
         send(part, part, AG_X(k, h, 1, 0), at_x(3))
@@ -234,6 +234,15 @@
             lanes = slice(head * HEAD, (head + 1) * HEAD)
             c = cots[part, lanes].astype(f32)
             centred[part, lanes] = c - jnp.sum(c, axis=1, keepdims=True) * (1.0 / HEAD)
+
+    def piece(step, part):
+        lanes = pl.ds(pl.multiple_of((x + step) % 4 * PIECE, PIECE), PIECE)
+        return lax.dot_general(
+            pat[part, lanes], dq[part, :], (((0,), (0,)), ((), ())), preferred_element_type=f32
+        )
+
+    near = rows(sh // 8 * (REPLICA // 2), REPLICA // 2, REPLICA // 2)
+    beyond = rows((1 - sh // 8) * (REPLICA // 2), REPLICA // 2, REPLICA // 2)
 
     def z4_pass(q):
         arrived(pat.at[rows(home(1) * BLOCK + q * 32, 32, 32)], Z4_SEM(q))
@@ -267,8 +276,12 @@
     shared_last(0)
     block_of(0, 2)
     y_forward(1, 0)
+    two[...] = piece(2, near)
+    plus[...] = piece(1, near)
     z4_pass(2)
     y_forward(1, 1)
+    minus[...] = piece(3, near)
+    mine[...] = piece(0, near)
     z4_pass(3)
     share(1, 0, 0)
     y_forward(1, 2)
@@ -287,12 +300,6 @@
     shared_last(1)
     block_of(1, 2)
 
-    def piece(step):
-        lanes = pl.ds(pl.multiple_of((x + step) % 4 * PIECE, PIECE), PIECE)
-        return lax.dot_general(
-            pat[:, lanes], dq[...], (((0,), (0,)), ((), ())), preferred_element_type=f32
-        )
-
     ORDER = (2, 1, 3, 0)
 
     def scatter_two(k, h):
@@ -334,13 +341,18 @@
         return total
 
     def scatter_start(k):
-        b_two[...] = piece(2).astype(bf16)
+        def add(ref, step):
+            if k == 0:
+                return ref[...] + piece(step, beyond)
+            return piece(step, pl.ds(0, REPLICA))
+
+        b_two[...] = add(two, 2).astype(bf16)
         for h in range(CUTS):
             scatter_two(k, h)
-        plus[...] = piece(1)
-        minus[...] = piece(3)
+        plus[...] = add(plus, 1)
+        minus[...] = add(minus, 3)
         scatter_x(k, 0)
-        mine[...] = piece(0)
+        mine[...] = add(mine, 0)
         for h in range(1, CUTS):
             scatter_x(k, h)
 
@@ -471,6 +483,7 @@
             pltpu.VMEM((PIECE, COLS), f32),
             pltpu.VMEM((PIECE, COLS), f32),
             pltpu.VMEM((PIECE, COLS), f32),
+            pltpu.VMEM((PIECE, COLS), f32),
             pltpu.VMEM((PIECE, COLS), bf16),
             pltpu.VMEM((PIECE, COLS), bf16),
             pltpu.VMEM((PIECE, COLS), bf16),

time: 165 us -> 164 us (level)
  no operation moved by 1% of the time
where the time goes in v4:
time: 164 us
  Pallas kernels  160 us (98%)
  local copies, waits for them, and re-layouts  3.17 us (2%)
    pallas_call x1, Pallas kernels, on_device(): pl.pallas_call(kernel, name='sam_step', out_shape=(pltpu.VMEM((D, COLS),...  160 us

profile of v4, /device:TPU:8, one launch (start us, length us, event | category | flops | bytes accessed | tf_op | source)
XLA Modules:
  0.0 163.9 jit_solution(12828043776194887271)
XLA Ops:
  0.6 160.1 %sam_step.1 = (bf16[3072,256]{1,0:T(8,128)(2,1)S(1)}, f32[192,256]{1,0:T(8,128)S(1)}, f32[192,256]{1,0:T(8,128)S(1)}, f32[192,256]{1,0:T(8,128)S(1)}) custom-call(bf16[128,3072]{1,0:T(8,128)(2,1)} %patches.1, bf16[2048,256]{1,0:T(8,128)(2,1)} %cot.1, f32[192,256]{1,0:T(8,128)} %master_in.1, f32[192,256]{1,0:T(8,128)} %moment_in.1, f32[192,256]{1,0:T(8,128)} %second_in.1), custom_call_target="tpu_custom_call" | custom-call | tf_op jit(solution)/shard_map/sam_step/pallas_call | solution.py:466
  160.7 1.1 copy.13
  161.9 0.7 copy.14
  162.5 0.7 copy.15
  163.2 0.7 copy.16
